TPU v7x, 32 devices: a whole 2x2x4 slice. The times are simulated.
32 devices in a mesh: row: 4 (over x, core), col: 8 (over z, y).
Axes of the slice: x: 2, y: 2, z: 4, core: 2. Of those that a mesh axis runs over, the one named last changes fastest.
Arguments:
- covariance: float32 [8192, 8192], P('row', 'col'), may hold values from -12 to 12, as said below
- noise_var: float32 [64, 128], P('row'), may hold values from 0.1 to 1
- wind_table: float32 [16, 2], replicated, may hold values from -0.7 to 0.7
- diffusivity: float32 [16], replicated, may hold values from 0.01 to 0.05
- wind_index: int32 [3, 64], replicated, may hold values from 0 to 15
Outputs:
- predicted_spread_matrix: float32 [8192, 8192], P('row', 'col')
- operator_times_prior: bfloat16 [8192, 8192], P('row', 'col')
Inputs may be any that keep to these rules, and one draw needn't show every extreme that they name: covariance is symmetric: entry (a, b) equals entry (b, a) exactly.
All inputs are finite; a program needn't handle non-finite values.
Results may differ from a plain program's by a relative error of at most 0.0025.
Values may be sent and summed in bfloat16 or wider, within the bound.
No kernel may reach another device: no remote copies, remote signals or barrier semaphores. Data moves between devices by JAX's collectives and lax.ppermute only.
A program may use at most 192 MiB of HBM per device.

v0:
```python
import functools

import jax
import jax.numpy as jnp
from jax import lax
from jax.experimental import pallas as pl
from jax.experimental.pallas import tpu as pltpu
from jax.sharding import PartitionSpec as P

F32 = jnp.float32
BF16 = jnp.bfloat16
VMEM_LIMIT = 63 * 1024 * 1024


def params():
    return pltpu.CompilerParams(vmem_limit_bytes=VMEM_LIMIT)


def cost(work):
    return pl.CostEstimate(flops=work, bytes_accessed=work, transcendentals=0)


def stencil_terms(zonal_cour, merid_cour, diffuse):
    middle_weight = 1.0 - zonal_cour * zonal_cour - merid_cour * merid_cour - 4.0 * diffuse
    eastward_weight = 0.5 * zonal_cour * zonal_cour - 0.5 * zonal_cour + diffuse
    west_w = 0.5 * zonal_cour * zonal_cour + 0.5 * zonal_cour + diffuse
    north_w = 0.5 * merid_cour * merid_cour - 0.5 * merid_cour + diffuse
    south_w = 0.5 * merid_cour * merid_cour + 0.5 * merid_cour + diffuse
    return jnp.stack([middle_weight, eastward_weight, west_w, north_w, south_w])


def looked_up(wind_table, diffusivity, wind_index):
    table_ids = jnp.arange(wind_table.shape[0], dtype=jnp.int32)
    one_hot = (wind_index[:, :, None] == table_ids[None, None, :]).astype(F32)
    courant = jnp.einsum("sly,yc->slc", one_hot, wind_table, precision=lax.Precision.HIGHEST)
    diffuse = jnp.einsum("sly,y->sl", one_hot, diffusivity, precision=lax.Precision.HIGHEST)
    return stencil_terms(courant[..., 0], courant[..., 1], diffuse)


def sweep(source, lats, weight, steps, axis, scratch, out):
    for step_no in range(steps):
        last = step_no == steps - 1
        target = out if last else scratch[step_no]
        south, here = source(0), source(1)
        size = here.shape[axis]
        for i in range(lats + 2 * (steps - step_no - 1)):
            north = source(i + 2)
            c, e, w, n, s = [weight(member, step_no, i + 1 + step_no) for member in range(5)]
            fresh = (
                c * here
                + e * pltpu.roll(here, size - 1, axis)
                + w * pltpu.roll(here, 1, axis)
                + n * north
                + s * south
            )
            target(i, fresh)
            south, here = here, north
        if not last:
            source = scratch[step_no]


def plane_view(ref, axis, size):
    def view(i, value=None):
        at = pl.ds(i * size, size)
        index = (at, slice(None)) if axis == 0 else (slice(None), at)
        if value is None:
            return ref[index].astype(F32)
        ref[index] = value.astype(ref.dtype)

    return view


def joined(before, middle, after, steps, lats):
    def view(i):
        if i < steps:
            return before(i)
        if i < steps + lats:
            return middle(i - steps)
        return after(i - steps - lats)

    return view


def edge_at(i, near, own):
    return jnp.where(i < near, i, i + own)


def pack_direct(covariance, where, near, own, halo, nlon):
    rows, cols = covariance.shape
    lat_rows = rows // nlon
    wide = halo * nlon
    count = 2 * near + own

    def kernel(where_ref, p_ref, last_ref, outer_ref, inner_ref, top_ref, bottom_ref):
        i = pl.program_id(0)
        inner = jnp.logical_and(i >= near, i < near + own)
        last_ref[...] = p_ref[:, cols - wide :].astype(BF16)

        @pl.when(jnp.logical_not(inner))
        def _():
            outer_ref[...] = p_ref[:, :wide].astype(BF16)

        @pl.when(inner)
        def _():
            inner_ref[...] = p_ref[:, :wide].astype(BF16)

        @pl.when(i < halo)
        def _():
            top_ref[...] = p_ref[...].astype(BF16)

        @pl.when(i >= count - halo)
        def _():
            bottom_ref[...] = p_ref[...].astype(BF16)

    def lat_at(i, at):
        inner = at[0] + i - near
        outer = jnp.where(i < near, i, i + lat_rows - count)
        return (jnp.where(jnp.logical_and(i >= near, i < near + own), inner, outer), 0)

    def outer_at(i, at):
        return (jnp.where(i < near, i, jnp.maximum(i - own, near - 1)), 0)

    return pl.pallas_call(
        kernel,
        grid_spec=pltpu.PrefetchScalarGridSpec(
            num_scalar_prefetch=1,
            grid=(count,),
            in_specs=[pl.BlockSpec((nlon, cols), lat_at)],
            out_specs=[
                pl.BlockSpec((nlon, wide), lambda i, at: (i, 0)),
                pl.BlockSpec((nlon, wide), outer_at),
                pl.BlockSpec((nlon, wide), lambda i, at: (jnp.clip(i - near, 0, own - 1), 0)),
                pl.BlockSpec((nlon, cols), lambda i, at: (jnp.minimum(i, halo - 1), 0)),
                pl.BlockSpec((nlon, cols), lambda i, at: (jnp.maximum(i - (count - halo), 0), 0)),
            ],
        ),
        out_shape=[
            jax.ShapeDtypeStruct((count * nlon, wide), BF16),
            jax.ShapeDtypeStruct((2 * near * nlon, wide), BF16),
            jax.ShapeDtypeStruct((own * nlon, wide), BF16),
            jax.ShapeDtypeStruct((wide, cols), BF16),
            jax.ShapeDtypeStruct((wide, cols), BF16),
        ],
        compiler_params=params(),
        cost_estimate=cost(1),
        name="pack_direct",
    )(where, covariance)


def pack_mirror(covariance, where, own, halo, nlon):
    rows, cols = covariance.shape
    wide = halo * nlon

    def kernel(where_ref, left_ref, right_ref, left_out, right_out):
        start = where_ref[2]
        for a in range(own):
            lanes = pl.ds(pl.multiple_of((start + a) * nlon, nlon), nlon)
            out_rows = pl.ds(a * nlon, nlon)
            left_out[out_rows, :] = left_ref[:, lanes].T.astype(BF16)
            right_out[out_rows, :] = right_ref[:, lanes].T.astype(BF16)

    return pl.pallas_call(
        kernel,
        grid_spec=pltpu.PrefetchScalarGridSpec(
            num_scalar_prefetch=1,
            grid=(halo,),
            in_specs=[
                pl.BlockSpec((nlon, cols), lambda j, at: (at[0] + j, 0)),
                pl.BlockSpec((nlon, cols), lambda j, at: (at[1] + j, 0)),
            ],
            out_specs=[
                pl.BlockSpec((own * nlon, nlon), lambda j, at: (0, j)),
                pl.BlockSpec((own * nlon, nlon), lambda j, at: (0, j)),
            ],
        ),
        out_shape=[jax.ShapeDtypeStruct((own * nlon, wide), BF16)] * 2,
        compiler_params=params(),
        cost_estimate=cost(1),
        name="pack_mirror",
    )(where, covariance, covariance)


def columns_operator(
    covariance, left, right, weights, where, steps, nlon, count, lat_at, left_at, right_at, held=None, work=1
):
    rows, cols = covariance.shape
    lats = cols // nlon
    wide = steps * nlon
    padded = lats + 2 * steps

    def kernel(where_ref, weight_ref, p_ref, left_ref, right_ref, *rest):
        outs = rest[: len(rest) - (steps - 1)] if held is None else rest[1 : len(rest) - (steps - 1)]
        scratch = rest[len(rest) - (steps - 1) :]
        t_ref = outs[0]

        def weight(member, step_no, lat):
            return weight_ref[(member * steps + step_no) * padded + lat]

        view = lambda ref: plane_view(ref, 1, nlon)
        source = joined(view(left_ref), view(p_ref), view(right_ref), steps, lats)
        sweep(source, lats, weight, steps, 1, [view(ref) for ref in scratch], view(t_ref))
        if held is None:
            i = pl.program_id(0)

            @pl.when(i < steps)
            def _():
                outs[1][...] = t_ref[...]

            @pl.when(i >= count - steps)
            def _():
                outs[2][...] = t_ref[...]

    in_specs = [
        pl.BlockSpec(memory_space=pltpu.SMEM),
        pl.BlockSpec((nlon, cols), lambda i, at: (lat_at(i, at), 0)),
        pl.BlockSpec((nlon, wide), lambda i, at: (left_at(i), 0)),
        pl.BlockSpec((nlon, wide), lambda i, at: (right_at(i), 0)),
    ]
    out_specs = [pl.BlockSpec((nlon, cols), lambda i, at: (lat_at(i, at), 0))]
    out_shape = [jax.ShapeDtypeStruct((rows, cols), BF16)]
    operands = [where, weights, covariance, left, right]
    aliases = {}
    if held is None:
        out_specs += [
            pl.BlockSpec((nlon, cols), lambda i, at: (jnp.minimum(i, steps - 1), 0)),
            pl.BlockSpec((nlon, cols), lambda i, at: (jnp.maximum(i - (count - steps), 0), 0)),
        ]
        out_shape += [jax.ShapeDtypeStruct((wide, cols), BF16)] * 2
    else:
        in_specs.append(pl.BlockSpec(memory_space=pl.ANY))
        operands.append(held)
        aliases = {5: 0}
    return pl.pallas_call(
        kernel,
        grid_spec=pltpu.PrefetchScalarGridSpec(
            num_scalar_prefetch=1,
            grid=(count,),
            in_specs=in_specs,
            out_specs=out_specs,
            scratch_shapes=[
                pltpu.VMEM((nlon, (padded - 2 * (step_no + 1)) * nlon), F32) for step_no in range(steps - 1)
            ],
        ),
        out_shape=out_shape,
        input_output_aliases=aliases,
        compiler_params=params(),
        cost_estimate=cost(work),
        name="columns_operator",
    )(*operands)


def rows_operator(values, top, bottom, weights, steps, nlon, out_dtype, noise=None, diagonal=None):
    rows, cols = values.shape
    lat_rows = rows // nlon
    wide = steps * nlon
    padded = lat_rows + 2 * steps

    def kernel(weight_ref, x_ref, top_ref, bottom_ref, *rest):
        extra, (out_ref, *scratch) = rest[: 0 if noise is None else 2], rest[0 if noise is None else 2 :]

        def weight(member, step_no, lat):
            return weight_ref[(member * steps + step_no) * padded + lat]

        view = lambda ref: plane_view(ref, 0, nlon)
        source = joined(view(top_ref), view(x_ref), view(bottom_ref), steps, lat_rows)
        sweep(source, lat_rows, weight, steps, 0, [view(ref) for ref in scratch], view(out_ref))

        if noise is not None:
            diagonal_ref, noise_ref = extra
            lat = diagonal_ref[0] + pl.program_id(0)

            @pl.when(jnp.logical_and(lat >= 0, lat < lat_rows))
            def _():
                at = pl.ds(pl.multiple_of(lat * nlon, nlon), nlon)
                eye = lax.broadcasted_iota(jnp.int32, (nlon, nlon), 0) == lax.broadcasted_iota(
                    jnp.int32, (nlon, nlon), 1
                )
                out_ref[at, :] += jnp.where(eye, noise_ref[pl.ds(lat, 1), :], 0.0)

    in_specs = [
        pl.BlockSpec(memory_space=pltpu.SMEM),
        pl.BlockSpec((rows, nlon), lambda j: (0, j)),
        pl.BlockSpec((wide, nlon), lambda j: (0, j)),
        pl.BlockSpec((wide, nlon), lambda j: (0, j)),
    ]
    operands = [weights, values, top, bottom]
    if noise is not None:
        in_specs += [pl.BlockSpec(memory_space=pltpu.SMEM), pl.BlockSpec(noise.shape, lambda j: (0, 0))]
        operands += [diagonal, noise]
    return pl.pallas_call(
        kernel,
        grid=(cols // nlon,),
        in_specs=in_specs,
        out_specs=pl.BlockSpec((rows, nlon), lambda j: (0, j)),
        out_shape=jax.ShapeDtypeStruct((rows, cols), out_dtype),
        scratch_shapes=[
            pltpu.VMEM(((padded - 2 * (step_no + 1)) * nlon, nlon), F32) for step_no in range(steps - 1)
        ],
        compiler_params=params(),
        cost_estimate=cost(1),
        name="rows_operator",
    )(*operands)


def shifted(block, axis, by):
    size = lax.axis_size(axis)
    pairs = [(i, i + by) for i in range(size) if 0 <= i + by < size]
    return lax.ppermute(block, axis, pairs)


def gathered(first, last, axis, dim, unit, halo, own):
    before, after = [], []
    need, hop = halo, 1
    while need > 0:
        take = min(own, need)
        size = first.shape[dim]
        before.insert(0, shifted(lax.slice_in_dim(last, size - take * unit, size, axis=dim), axis, hop))
        after.append(shifted(lax.slice_in_dim(first, 0, take * unit, axis=dim), axis, -hop))
        need, hop = need - take, hop + 1
    join = lambda parts: parts[0] if len(parts) == 1 else jnp.concatenate(parts, axis=dim)
    return join(before), join(after)


def mirror_pairs(n_row, n_col, side):
    pairs = []
    for a in range(n_row):
        for b in range(n_col):
            to = 2 * a + (1 - b % 2) + side
            if 0 <= to < n_col:
                pairs.append((a * n_col + b, (b // 2) * n_col + to))
    return pairs


def body(covariance, noise_var, wind_table, diffusivity, wind_index):
    rows_dev, cols_dev = covariance.shape
    lat_rows, nlon = noise_var.shape
    steps, nlat = wind_index.shape
    lats = cols_dev // nlon
    n_row, n_col = lax.axis_size("row"), lax.axis_size("col")
    row_id, col_id = lax.axis_index("row"), lax.axis_index("col")
    own = min(lats - steps, lat_rows // 2 - steps, lats // 2)
    mirrored = lat_rows == 2 * lats and own > 0

    if not mirrored:
        return plain_body(covariance, noise_var, wind_table, diffusivity, wind_index)

    near = lat_rows // 2 - own
    middle = lat_rows // 2
    parity = col_id % 2
    by_parity = lambda even, odd: jnp.where(parity == 0, even, odd).astype(jnp.int32)
    mirror_at = by_parity(middle - own, middle).reshape(1)
    direct_at = by_parity(middle, middle - own).reshape(1)
    last, first_outer, first_inner, top, bottom = pack_direct(covariance, mirror_at, near, own, steps, nlon)
    left = shifted(last, "col", 1)
    right_outer = shifted(first_outer, "col", -1)
    p_top = shifted(bottom, "row", 1)
    p_bottom = shifted(top, "row", -1)

    base = (1 - parity) * lats
    sources = jnp.stack([base + lats - steps, base, by_parity(lats - own, 0)]).astype(jnp.int32)
    sources, top = lax.optimization_barrier((sources, top))
    left_m, right_m = pack_mirror(covariance, sources, own, steps, nlon)
    left_m, right_m, first_inner, wind_index, p_top, p_bottom = lax.optimization_barrier(
        (left_m, right_m, first_inner, wind_index, p_top, p_bottom)
    )
    left_m = lax.ppermute(left_m, ("row", "col"), mirror_pairs(n_row, n_col, 1))
    right_m = lax.ppermute(right_m, ("row", "col"), mirror_pairs(n_row, n_col, -1))
    right_inner = shifted(first_inner, "col", -1)

    weights = looked_up(wind_table, diffusivity, wind_index)
    padded_w = jnp.pad(weights, ((0, 0), (0, 0), (steps, steps)))
    row_w = lax.dynamic_slice_in_dim(padded_w, row_id * lat_rows, lat_rows + 2 * steps, 2).reshape(-1)
    col_w = lax.dynamic_slice_in_dim(padded_w, col_id * lats, lats + 2 * steps, 2).reshape(-1)

    operator_times_prior = rows_operator(covariance, p_top, p_bottom, row_w, steps, nlon, BF16)
    operator_times_prior, right_outer = lax.optimization_barrier((operator_times_prior, right_outer))
    same = lambda i: i
    inner_at = lambda i, at: at[0] + i
    mirror, t_first, t_last = columns_operator(
        covariance, left, right_outer, col_w, mirror_at, steps, nlon, 2 * near,
        lambda i, at: edge_at(i, near, 2 * own), lambda i: edge_at(i, near, own), same,
    )
    t_top = shifted(t_last, "row", 1)
    t_bottom = shifted(t_first, "row", -1)
    (mirror,) = columns_operator(
        covariance, left_m, right_m, col_w, mirror_at, steps, nlon, own, inner_at, same, same, mirror
    )
    (mirror,) = columns_operator(
        covariance, left, right_inner, col_w, direct_at, steps, nlon, own, inner_at,
        lambda i: i + near, same, mirror, 10 ** 13,
    )
    diagonal = (col_id * lats - row_id * lat_rows).astype(jnp.int32).reshape(1)
    predicted_spread_matrix = rows_operator(
        mirror, t_top, t_bottom, row_w, steps, nlon, F32, noise_var, diagonal
    )
    return (predicted_spread_matrix, operator_times_prior)


def plain_body(covariance, noise_var, wind_table, diffusivity, wind_index):
    rows_dev, cols_dev = covariance.shape
    lat_rows, nlon = noise_var.shape
    steps, nlat = wind_index.shape
    lats = cols_dev // nlon
    row_id, col_id = lax.axis_index("row"), lax.axis_index("col")
    sent = covariance.astype(BF16)
    left, right = gathered(sent, sent, "col", 1, nlon, steps, lats)
    p_top, p_bottom = gathered(sent, sent, "row", 0, nlon, steps, lat_rows)
    weights = looked_up(wind_table, diffusivity, wind_index)
    padded_w = jnp.pad(weights, ((0, 0), (0, 0), (steps, steps)))
    row_w = lax.dynamic_slice_in_dim(padded_w, row_id * lat_rows, lat_rows + 2 * steps, 2).reshape(-1)
    col_w = lax.dynamic_slice_in_dim(padded_w, col_id * lats, lats + 2 * steps, 2).reshape(-1)
    operator_times_prior = rows_operator(covariance, p_top, p_bottom, row_w, steps, nlon, BF16)
    unused = jnp.zeros((1,), jnp.int32)
    held = jnp.zeros((rows_dev, cols_dev), BF16)
    same = lambda i: i
    (mirror,) = columns_operator(
        covariance, left, right, col_w, unused, steps, nlon, lat_rows, lambda i, at: i, same, same, held
    )
    t_top, t_bottom = gathered(mirror, mirror, "row", 0, nlon, steps, lat_rows)
    diagonal = (col_id * lats - row_id * lat_rows).astype(jnp.int32).reshape(1)
    predicted_spread_matrix = rows_operator(
        mirror, t_top, t_bottom, row_w, steps, nlon, F32, noise_var, diagonal
    )
    return (predicted_spread_matrix, operator_times_prior)


def solution(mesh):
    in_specs = (P("row", "col"), P("row", None), P(), P(), P())
    out_specs = (P("row", "col"), P("row", "col"))
    return jax.shard_map(body, mesh=mesh, in_specs=in_specs, out_specs=out_specs, check_vma=False)
```

profile of v0, /device:TPU:5, one launch (start us, length us, event | category | flops | bytes accessed | tf_op | source)
XLA Modules:
  0.0 117.0 jit_solution(15224586294046426575)
XLA Ops:
  0.6 0.0 copy-start
  0.7 9.1 %pack_direct.1 = (bf16[1536,384]{1,0:T(8,128)(2,1)}, bf16[1024,384]{1,0:T(8,128)(2,1)}, bf16[512,384]{1,0:T(8,128)(2,1)}, bf16[384,1024]{1,0:T(8,128)(2,1)}, bf16[384,1024]{1,0:T(8,128)(2,1)}) custom-call(s32[1]{0:T(128)} %bitcast.3.where_ref, f32[2048,1024]{1,0:T(8,128)} %p_ref.7), custom_call_target="tpu_custom_call" | custom-call | flops 1 | bytes 1 | tf_op jit(solution)/shard_map/pack_direct/pallas_call | solution.py:123
  9.7 3.7 %collective-permute-start = (bf16[384,1024]{1,0:T(8,128)(2,1)}, bf16[384,1024]{1,0:T(8,128)(2,1)}, u32[]{:S(2)}, u32[]{:S(2)}) collective-permute-start(bf16[384,1024]{1,0:T(8,128)(2,1)} %get-tuple-element.26), channel_id=1, source_target_pairs={{0,8},{8,16},{16,24},{1,9},{9,17},{17,25},{2,10},{10,18},{18,26},{... | collective-permute-start | bytes 2359304 | tf_op jit(solution)/shard_map/ppermute | solution.py:308
  13.4 1.9 %collective-permute-start.1 = (bf16[384,1024]{1,0:T(8,128)(2,1)}, bf16[384,1024]{1,0:T(8,128)(2,1)}, u32[]{:S(2)}, u32[]{:S(2)}) collective-permute-start(bf16[384,1024]{1,0:T(8,128)(2,1)} %get-tuple-element.21), channel_id=1, source_target_pairs={{8,0},{16,8},{24,16},{9,1},{17,9},{25,17},{10,2},{18,10},{26,18},{... | collective-permute-start | bytes 2359304 | tf_op jit(solution)/shard_map/ppermute | solution.py:308
  15.3 2.1 %collective-permute-start.6 = (bf16[1024,384]{1,0:T(8,128)(2,1)}, bf16[1024,384]{1,0:T(8,128)(2,1)S(1)}, u32[]{:S(2)}, u32[]{:S(2)}) collective-permute-start(bf16[1024,384]{1,0:T(8,128)(2,1)} %get-tuple-element.34), channel_id=1, source_target_pairs={{1,0},{2,1},{3,2},{4,3},{5,4},{6,5},{7,6},{9,8},{10,9},{11,10},{12... | collective-permute-start | bytes 2359304 | tf_op jit(solution)/shard_map/ppermute | solution.py:308
  17.5 4.0 %collective-permute-start.2 = (bf16[1536,384]{1,0:T(8,128)(2,1)}, bf16[1536,384]{1,0:T(8,128)(2,1)}, u32[]{:S(2)}, u32[]{:S(2)}) collective-permute-start(bf16[1536,384]{1,0:T(8,128)(2,1)} %get-tuple-element.28), channel_id=1, source_target_pairs={{0,1},{1,2},{2,3},{3,4},{4,5},{5,6},{6,7},{8,9},{9,10},{10,11},{11... | collective-permute-start | bytes 3538952 | tf_op jit(solution)/shard_map/ppermute | solution.py:308
  21.5 0.6 pad_add_fusion.where_ref
  22.1 0.0 copy-start.2
  22.1 0.0 copy-start.3
  22.1 4.5 %pack_mirror.1 = (bf16[512,384]{1,0:T(8,128)(2,1)}, bf16[512,384]{1,0:T(8,128)(2,1)}) custom-call(s32[3]{0:T(128)} %pad_add_fusion.where_ref, f32[2048,1024]{1,0:T(8,128)} %p_ref.7, f32[2048,1024]{1,0:T(8,128)} %p_ref.7), custom_call_target="tpu_custom_call" | custom-call | flops 1 | bytes 1 | tf_op jit(solution)/shard_map/pack_mirror/pallas_call | solution.py:162
  26.6 0.0 collective-permute-done.top_ref
  26.6 0.7 collective-permute-done.1.bottom_ref
  27.3 0.0 copy-done.2
  27.3 0.0 copy-done.3
  27.3 0.1 fusion
  27.5 0.0 copy-done
  27.5 0.1 fusion.1
  27.6 2.0 %collective-permute-start.3 = (bf16[512,384]{1,0:T(8,128)(2,1)}, bf16[512,384]{1,0:T(8,128)(2,1)}, u32[]{:S(2)}, u32[]{:S(2)}) collective-permute-start(bf16[512,384]{1,0:T(8,128)(2,1)} %get-tuple-element.29), channel_id=1, source_target_pairs={{1,0},{2,1},{3,2},{4,3},{5,4},{6,5},{7,6},{9,8},{10,9},{11,10},{12... | collective-permute-start | bytes 1179656 | tf_op jit(solution)/shard_map/ppermute | solution.py:308
  29.6 1.9 %collective-permute-start.4 = (bf16[512,384]{1,0:T(8,128)(2,1)}, bf16[512,384]{1,0:T(8,128)(2,1)}, u32[]{:S(2)}, u32[]{:S(2)}) collective-permute-start(bf16[512,384]{1,0:T(8,128)(2,1)} %get-tuple-element.30), channel_id=1, source_target_pairs={{0,2},{1,1},{2,10},{3,9},{4,18},{5,17},{6,26},{7,25},{8,4},{9,3},{... | collective-permute-start | bytes 1179656 | tf_op jit(solution)/shard_map/ppermute | solution.py:366
  31.6 3.4 %collective-permute-start.5 = (bf16[512,384]{1,0:T(8,128)(2,1)}, bf16[512,384]{1,0:T(8,128)(2,1)}, u32[]{:S(2)}, u32[]{:S(2)}) collective-permute-start(bf16[512,384]{1,0:T(8,128)(2,1)} %get-tuple-element.31), channel_id=1, source_target_pairs={{0,0},{2,8},{4,16},{6,24},{8,2},{9,1},{10,10},{11,9},{12,18},{13,1... | collective-permute-start | bytes 1179656 | tf_op jit(solution)/shard_map/ppermute | solution.py:367
  35.0 0.1 pad_dynamic-slice_fusion.1
  35.1 0.6 reshape.21.weight_ref
  35.7 15.7 %rows_operator.2 = bf16[2048,1024]{1,0:T(8,128)(2,1)} custom-call(f32[330]{0:T(512)} %reshape.21.weight_ref, f32[2048,1024]{1,0:T(8,128)} %p_ref.7, bf16[384,1024]{1,0:T(8,128)(2,1)} %collective-permute-done.top_ref, bf16[384,1024]{1,0:T(8,128)(2,1)} %collective-permute-done.1.bottom_ref), custom_call_target="tpu_custom_call" | custom-call | flops 1 | bytes 1 | tf_op jit(solution)/shard_map/rows_operator/pallas_call | solution.py:290
  51.4 0.1 pad_dynamic-slice_fusion
  51.5 0.7 reshape.23.weight_ref
  52.2 0.0 collective-permute-done.6.right_ref
  52.2 0.0 copy-start.1
  52.2 18.9 %collective-permute-done.2.left_ref = bf16[1536,384]{1,0:T(8,128)(2,1)} collective-permute-done((bf16[1536,384]{1,0:T(8,128)(2,1)}, bf16[1536,384]{1,0:T(8,128)(2,1)}, u32[]{:S(2)}, u32[]{:S(2)}) %collective-permute-start.2) | collective-permute-done | bytes 1179680 | tf_op jit(solution)/shard_map/ppermute | solution.py:308
  71.1 0.0 copy-done.1
  71.1 11.7 %columns_operator.3 = (bf16[2048,1024]{1,0:T(8,128)(2,1)}, bf16[384,1024]{1,0:T(8,128)(2,1)}, bf16[384,1024]{1,0:T(8,128)(2,1)}) custom-call(s32[1]{0:T(128)} %bitcast.3.where_ref, f32[210]{0:T(256)} %reshape.23.weight_ref, f32[2048,1024]{1,0:T(8,128)} %p_ref.7, bf16[1536,384]{1,0:T(8,128)(2,1)} %collective-permute-done.2.left_ref, bf16[1024,384]{1,0:T(8,128)(2,1)} %copy-done.1), custom_call_target="tpu_custom_call" | custom-call | flops 1 | bytes 1 | tf_op jit(solution)/shard_map/columns_operator/pallas_call | solution.py:233
  82.8 3.8 %collective-permute-start.7 = (bf16[384,1024]{1,0:T(8,128)(2,1)}, bf16[384,1024]{1,0:T(8,128)(2,1)}, u32[]{:S(2)}, u32[]{:S(2)}) collective-permute-start(bf16[384,1024]{1,0:T(8,128)(2,1)} %get-tuple-element.37), channel_id=1, source_target_pairs={{0,8},{8,16},{16,24},{1,9},{9,17},{17,25},{2,10},{10,18},{18,26},{... | collective-permute-start | bytes 2359304 | tf_op jit(solution)/shard_map/ppermute | solution.py:308
  86.6 1.9 %collective-permute-start.8 = (bf16[384,1024]{1,0:T(8,128)(2,1)}, bf16[384,1024]{1,0:T(8,128)(2,1)}, u32[]{:S(2)}, u32[]{:S(2)}) collective-permute-start(bf16[384,1024]{1,0:T(8,128)(2,1)} %get-tuple-element.38), channel_id=1, source_target_pairs={{8,0},{16,8},{24,16},{9,1},{17,9},{25,17},{10,2},{18,10},{26,18},{... | collective-permute-start | bytes 2359304 | tf_op jit(solution)/shard_map/ppermute | solution.py:308
  88.5 0.0 collective-permute-done.4.left_ref
  88.6 0.0 collective-permute-done.5.right_ref
  88.6 6.5 %columns_operator.4.rest_0_ = bf16[2048,1024]{1,0:T(8,128)(2,1)} custom-call(s32[1]{0:T(128)} %bitcast.3.where_ref, f32[210]{0:T(256)} %reshape.23.weight_ref, f32[2048,1024]{1,0:T(8,128)} %p_ref.7, bf16[512,384]{1,0:T(8,128)(2,1)} %collective-permute-done.4.left_ref, ...), custom_call_target="tpu_custom_call", output_to_operand_aliasing={{}: (5, {})} | custom-call | flops 1 | bytes 1 | tf_op jit(solution)/shard_map/columns_operator/pallas_call | solution.py:233
  95.0 0.0 collective-permute-done.3.right_ref
  95.0 6.5 %columns_operator.5.x_ref = bf16[2048,1024]{1,0:T(8,128)(2,1)} custom-call(s32[1]{0:T(128)} %bitcast.13.where_ref, f32[210]{0:T(256)} %reshape.23.weight_ref, f32[2048,1024]{1,0:T(8,128)} %p_ref.7, bf16[1536,384]{1,0:T(8,128)(2,1)} %collective-permute-done.2.left_ref, ...), custom_call_target="tpu_custom_call", output_to_operand_aliasing={{}: (5, {})} | custom-call | flops 9999999827968 | bytes 9999999827968 | tf_op jit(solution)/shard_map/columns_operator/pallas_call | solution.py:233
  101.6 0.0 collective-permute-done.7.top_ref
  101.6 0.0 collective-permute-done.8.bottom_ref
  101.6 15.5 %rows_operator.3 = f32[2048,1024]{1,0:T(8,128)} custom-call(f32[330]{0:T(512)} %reshape.21.weight_ref, bf16[2048,1024]{1,0:T(8,128)(2,1)} %columns_operator.5.x_ref, bf16[384,1024]{1,0:T(8,128)(2,1)} %collective-permute-done.7.top_ref, bf16[384,1024]{1,0:T(8,128)(2,1)} %collective-permute-done.8.bottom_ref, s32[1]{0:T(128)} %bitcast.14.rest_0_, ...), custom_call_target="tpu_custom_call" | custom-call | flops 1 | bytes 1 | tf_op jit(solution)/shard_map/rows_operator/pallas_call | solution.py:290
  (6 shorter events, 0.1 us)
Async XLA Ops:
  0.6 26.8 %copy-start = (f32[16,2]{0,1:T(2,128)S(1)}, f32[16,2]{0,1:T(2,128)}, u32[]{:S(2)}) copy-start(f32[16,2]{0,1:T(2,128)} %param.7) | copy-start | bytes 388
  9.7 16.9 %collective-permute-start = (bf16[384,1024]{1,0:T(8,128)(2,1)}, bf16[384,1024]{1,0:T(8,128)(2,1)}, u32[]{:S(2)}, u32[]{:S(2)}) collective-permute-start(bf16[384,1024]{1,0:T(8,128)(2,1)} %get-tuple-element.26), channel_id=1, source_target_pairs={{0,8},{8,16},{16,24},{1,9},{9,17},{17,25},{2,10},{10,18},{18,26},{... | collective-permute-start | bytes 2359304 | tf_op jit(solution)/shard_map/ppermute | solution.py:308
  13.4 13.9 %collective-permute-start.1 = (bf16[384,1024]{1,0:T(8,128)(2,1)}, bf16[384,1024]{1,0:T(8,128)(2,1)}, u32[]{:S(2)}, u32[]{:S(2)}) collective-permute-start(bf16[384,1024]{1,0:T(8,128)(2,1)} %get-tuple-element.21), channel_id=1, source_target_pairs={{8,0},{16,8},{24,16},{9,1},{17,9},{25,17},{10,2},{18,10},{26,18},{... | collective-permute-start | bytes 2359304 | tf_op jit(solution)/shard_map/ppermute | solution.py:308
  15.3 36.8 %collective-permute-start.6 = (bf16[1024,384]{1,0:T(8,128)(2,1)}, bf16[1024,384]{1,0:T(8,128)(2,1)S(1)}, u32[]{:S(2)}, u32[]{:S(2)}) collective-permute-start(bf16[1024,384]{1,0:T(8,128)(2,1)} %get-tuple-element.34), channel_id=1, source_target_pairs={{1,0},{2,1},{3,2},{4,3},{5,4},{6,5},{7,6},{9,8},{10,9},{11,10},{12... | collective-permute-start | bytes 2359304 | tf_op jit(solution)/shard_map/ppermute | solution.py:308
  17.5 53.6 %collective-permute-start.2 = (bf16[1536,384]{1,0:T(8,128)(2,1)}, bf16[1536,384]{1,0:T(8,128)(2,1)}, u32[]{:S(2)}, u32[]{:S(2)}) collective-permute-start(bf16[1536,384]{1,0:T(8,128)(2,1)} %get-tuple-element.28), channel_id=1, source_target_pairs={{0,1},{1,2},{2,3},{3,4},{4,5},{5,6},{6,7},{8,9},{9,10},{10,11},{11... | collective-permute-start | bytes 3538952 | tf_op jit(solution)/shard_map/ppermute | solution.py:308
  22.1 5.2 %copy-start.2 = (s32[3,64]{1,0:T(4,128)S(1)}, s32[3,64]{1,0:T(4,128)}, u32[]{:S(2)}) copy-start(s32[3,64]{1,0:T(4,128)} %param.9) | copy-start | bytes 2308
  22.1 5.2 %copy-start.3 = (f32[16]{0:T(128)S(1)}, f32[16]{0:T(128)}, u32[]{:S(2)}) copy-start(f32[16]{0:T(128)} %param.8) | copy-start | bytes 196
  27.6 67.4 %collective-permute-start.3 = (bf16[512,384]{1,0:T(8,128)(2,1)}, bf16[512,384]{1,0:T(8,128)(2,1)}, u32[]{:S(2)}, u32[]{:S(2)}) collective-permute-start(bf16[512,384]{1,0:T(8,128)(2,1)} %get-tuple-element.29), channel_id=1, source_target_pairs={{1,0},{2,1},{3,2},{4,3},{5,4},{6,5},{7,6},{9,8},{10,9},{11,10},{12... | collective-permute-start | bytes 1179656 | tf_op jit(solution)/shard_map/ppermute | solution.py:308
  29.6 58.9 %collective-permute-start.4 = (bf16[512,384]{1,0:T(8,128)(2,1)}, bf16[512,384]{1,0:T(8,128)(2,1)}, u32[]{:S(2)}, u32[]{:S(2)}) collective-permute-start(bf16[512,384]{1,0:T(8,128)(2,1)} %get-tuple-element.30), channel_id=1, source_target_pairs={{0,2},{1,1},{2,10},{3,9},{4,18},{5,17},{6,26},{7,25},{8,4},{9,3},{... | collective-permute-start | bytes 1179656 | tf_op jit(solution)/shard_map/ppermute | solution.py:366
  31.6 57.0 %collective-permute-start.5 = (bf16[512,384]{1,0:T(8,128)(2,1)}, bf16[512,384]{1,0:T(8,128)(2,1)}, u32[]{:S(2)}, u32[]{:S(2)}) collective-permute-start(bf16[512,384]{1,0:T(8,128)(2,1)} %get-tuple-element.31), channel_id=1, source_target_pairs={{0,0},{2,8},{4,16},{6,24},{8,2},{9,1},{10,10},{11,9},{12,18},{13,1... | collective-permute-start | bytes 1179656 | tf_op jit(solution)/shard_map/ppermute | solution.py:367
  52.2 18.9 %copy-start.1 = (bf16[1024,384]{1,0:T(8,128)(2,1)}, bf16[1024,384]{1,0:T(8,128)(2,1)S(1)}, u32[]{:S(2)}) copy-start(bf16[1024,384]{1,0:T(8,128)(2,1)S(1)} %collective-permute-done.6.right_ref) | copy-start | bytes 2359300
  82.8 18.7 %collective-permute-start.7 = (bf16[384,1024]{1,0:T(8,128)(2,1)}, bf16[384,1024]{1,0:T(8,128)(2,1)}, u32[]{:S(2)}, u32[]{:S(2)}) collective-permute-start(bf16[384,1024]{1,0:T(8,128)(2,1)} %get-tuple-element.37), channel_id=1, source_target_pairs={{0,8},{8,16},{16,24},{1,9},{9,17},{17,25},{2,10},{10,18},{18,26},{... | collective-permute-start | bytes 2359304 | tf_op jit(solution)/shard_map/ppermute | solution.py:308
  86.6 14.9 %collective-permute-start.8 = (bf16[384,1024]{1,0:T(8,128)(2,1)}, bf16[384,1024]{1,0:T(8,128)(2,1)}, u32[]{:S(2)}, u32[]{:S(2)}) collective-permute-start(bf16[384,1024]{1,0:T(8,128)(2,1)} %get-tuple-element.38), channel_id=1, source_target_pairs={{8,0},{16,8},{24,16},{9,1},{17,9},{25,17},{10,2},{18,10},{26,18},{... | collective-permute-start | bytes 2359304 | tf_op jit(solution)/shard_map/ppermute | solution.py:308
where the time goes:
time: 118 us; the launch traced here: 117 us
  Pallas kernels  69.4 us (59%)
  starting transfers between devices  24.8 us (21%)
  waiting for transfers between devices  19.7 us (17%)
  local copies, waits for them, and re-layouts  1.48 us (1%)
    pallas_call x2, Pallas kernels, rows_operator(): pl.pallas_call(kernel, grid=(cols // nlon,), in_specs=in_specs, out_specs...  31.1 us
    pallas_call x3, Pallas kernels, columns_operator(): pl.pallas_call(kernel, grid_spec=pltpu.PrefetchScalarGridSpec(num_scalar_...  24.7 us
    ppermute x7, waiting for transfers between devices, shifted(): return lax.ppermute(block, axis, pairs)  19.6 us
    ppermute x7, starting transfers between devices, shifted(): return lax.ppermute(block, axis, pairs)  19.5 us
    pallas_call x1, Pallas kernels, pack_direct(): pl.pallas_call(kernel, grid_spec=pltpu.PrefetchScalarGridSpec(num_scalar_...  9.06 us
    pallas_call x1, Pallas kernels, pack_mirror(): pl.pallas_call(kernel, grid_spec=pltpu.PrefetchScalarGridSpec(num_scalar_...  4.47 us
    ppermute x1, starting transfers between devices, body(): lax.ppermute(right_m, ('row', 'col'), mirror_pairs(n_row, n_col, -1))  3.39 us
  transfers between devices with their start and end apart: 9, of which 2 were waited for; matrix products, arithmetic and copies ran while one was open for 2% of the time, Pallas kernels for 38%

commit v1 on v0

--- a/solution.py
+++ b/solution.py
@@ -85,99 +85,69 @@
     return jnp.where(i < near, i, i + own)
 
 
-def pack_direct(covariance, where, near, own, halo, nlon):
+def pack(covariance, where, near, own, halo, nlon):
     rows, cols = covariance.shape
-    lat_rows = rows // nlon
     wide = halo * nlon
-    count = 2 * near + own
-
-    def kernel(where_ref, p_ref, last_ref, outer_ref, inner_ref, top_ref, bottom_ref):
-        i = pl.program_id(0)
-        inner = jnp.logical_and(i >= near, i < near + own)
-        last_ref[...] = p_ref[:, cols - wide :].astype(BF16)
-
-        @pl.when(jnp.logical_not(inner))
-        def _():
-            outer_ref[...] = p_ref[:, :wide].astype(BF16)
-
-        @pl.when(inner)
-        def _():
-            inner_ref[...] = p_ref[:, :wide].astype(BF16)
-
-        @pl.when(i < halo)
-        def _():
-            top_ref[...] = p_ref[...].astype(BF16)
-
-        @pl.when(i >= count - halo)
-        def _():
-            bottom_ref[...] = p_ref[...].astype(BF16)
-
-    def lat_at(i, at):
-        inner = at[0] + i - near
-        outer = jnp.where(i < near, i, i + lat_rows - count)
-        return (jnp.where(jnp.logical_and(i >= near, i < near + own), inner, outer), 0)
-
-    def outer_at(i, at):
-        return (jnp.where(i < near, i, jnp.maximum(i - own, near - 1)), 0)
+    outer, span = near * nlon, own * nlon
+    direct = [(0, outer, 0, 0), (0, outer, outer, rows - outer), (2, span, 0, None)]
+    made_shapes = [(2 * outer, wide)] * 2 + [(span, wide)] * 4 + [(wide, cols)] * 2
+    got_shapes = [(size, wide) for _, size, _, _ in direct for _ in range(2)]
+    got_shapes += [(wide, span)] * 2 + [(wide, cols)] * 2
+
+    def kernel(where_ref, p_ref, *refs):
+        outs, got, made, in_sem, out_sem = refs[:8], refs[8:18], refs[18:26], refs[26], refs[27]
+        lat = lambda k: pl.multiple_of(where_ref[k] * nlon, nlon)
+        sources = []
+        for _, size, _, start in direct:
+            at = pl.ds(lat(0) if start is None else start, size)
+            sources += [p_ref.at[at, pl.ds(lane, wide)] for lane in (0, cols - wide)]
+        sources += [p_ref.at[pl.ds(lat(k), wide), pl.ds(lat(3), span)] for k in (1, 2)]
+        sources += [p_ref.at[pl.ds(start, wide), :] for start in (0, rows - wide)]
+        loads = [
+            pltpu.make_async_copy(source, got[k], in_sem.at[k]) for k, source in enumerate(sources)
+        ]
+        for load in loads:
+            load.start()
+        stores = []
+
+        def store(k, row, size):
+            at = pl.ds(row, size)
+            stores.append(
+                pltpu.make_async_copy(made[k].at[at, :], outs[k].at[at, :], out_sem.at[len(stores)])
+            )
+            stores[-1].start()
+
+        for k, (first_out, size, row, _) in enumerate(direct):
+            for side in range(2):
+                loads[2 * k + side].wait()
+                made[first_out + side][row : row + size, :] = got[2 * k + side][...].astype(BF16)
+                store(first_out + side, row, size)
+        for k in range(2):
+            loads[6 + k].wait()
+            for j in range(halo):
+                for a in range(own):
+                    block = got[6 + k][j * nlon : (j + 1) * nlon, a * nlon : (a + 1) * nlon]
+                    made[4 + k][a * nlon : (a + 1) * nlon, j * nlon : (j + 1) * nlon] = block.T.astype(BF16)
+            store(4 + k, 0, span)
+        for k in range(2):
+            loads[8 + k].wait()
+            made[6 + k][...] = got[8 + k][...].astype(BF16)
+            store(6 + k, 0, wide)
+        for copy in stores:
+            copy.wait()
 
     return pl.pallas_call(
         kernel,
-        grid_spec=pltpu.PrefetchScalarGridSpec(
-            num_scalar_prefetch=1,
-            grid=(count,),
-            in_specs=[pl.BlockSpec((nlon, cols), lat_at)],
-            out_specs=[
-                pl.BlockSpec((nlon, wide), lambda i, at: (i, 0)),
-                pl.BlockSpec((nlon, wide), outer_at),
-                pl.BlockSpec((nlon, wide), lambda i, at: (jnp.clip(i - near, 0, own - 1), 0)),
-                pl.BlockSpec((nlon, cols), lambda i, at: (jnp.minimum(i, halo - 1), 0)),
-                pl.BlockSpec((nlon, cols), lambda i, at: (jnp.maximum(i - (count - halo), 0), 0)),
-            ],
-        ),
-        out_shape=[
-            jax.ShapeDtypeStruct((count * nlon, wide), BF16),
-            jax.ShapeDtypeStruct((2 * near * nlon, wide), BF16),
-            jax.ShapeDtypeStruct((own * nlon, wide), BF16),
-            jax.ShapeDtypeStruct((wide, cols), BF16),
-            jax.ShapeDtypeStruct((wide, cols), BF16),
-        ],
+        in_specs=[pl.BlockSpec(memory_space=pltpu.SMEM), pl.BlockSpec(memory_space=pl.ANY)],
+        out_specs=[pl.BlockSpec(memory_space=pl.ANY)] * 8,
+        out_shape=[jax.ShapeDtypeStruct(shape, BF16) for shape in made_shapes],
+        scratch_shapes=[pltpu.VMEM(shape, F32) for shape in got_shapes]
+        + [pltpu.VMEM(shape, BF16) for shape in made_shapes]
+        + [pltpu.SemaphoreType.DMA((10,)), pltpu.SemaphoreType.DMA((10,))],
         compiler_params=params(),
         cost_estimate=cost(1),
-        name="pack_direct",
+        name="pack",
     )(where, covariance)
-
-
-def pack_mirror(covariance, where, own, halo, nlon):
-    rows, cols = covariance.shape
-    wide = halo * nlon
-
-    def kernel(where_ref, left_ref, right_ref, left_out, right_out):
-        start = where_ref[2]
-        for a in range(own):
-            lanes = pl.ds(pl.multiple_of((start + a) * nlon, nlon), nlon)
-            out_rows = pl.ds(a * nlon, nlon)
-            left_out[out_rows, :] = left_ref[:, lanes].T.astype(BF16)
-            right_out[out_rows, :] = right_ref[:, lanes].T.astype(BF16)
-
-    return pl.pallas_call(
-        kernel,
-        grid_spec=pltpu.PrefetchScalarGridSpec(
-            num_scalar_prefetch=1,
-            grid=(halo,),
-            in_specs=[
-                pl.BlockSpec((nlon, cols), lambda j, at: (at[0] + j, 0)),
-                pl.BlockSpec((nlon, cols), lambda j, at: (at[1] + j, 0)),
-            ],
-            out_specs=[
-                pl.BlockSpec((own * nlon, nlon), lambda j, at: (0, j)),
-                pl.BlockSpec((own * nlon, nlon), lambda j, at: (0, j)),
-            ],
-        ),
-        out_shape=[jax.ShapeDtypeStruct((own * nlon, wide), BF16)] * 2,
-        compiler_params=params(),
-        cost_estimate=cost(1),
-        name="pack_mirror",
-    )(where, covariance, covariance)
 
 
 def columns_operator(
@@ -350,22 +320,18 @@
     by_parity = lambda even, odd: jnp.where(parity == 0, even, odd).astype(jnp.int32)
     mirror_at = by_parity(middle - own, middle).reshape(1)
     direct_at = by_parity(middle, middle - own).reshape(1)
-    last, first_outer, first_inner, top, bottom = pack_direct(covariance, mirror_at, near, own, steps, nlon)
+    base = (1 - parity) * lats
+    sources = jnp.stack([mirror_at[0], base + lats - steps, base, by_parity(lats - own, 0)]).astype(jnp.int32)
+    first, last, first_inner, last_inner, left_m, right_m, top, bottom = pack(
+        covariance, sources, near, own, steps, nlon
+    )
     left = shifted(last, "col", 1)
-    right_outer = shifted(first_outer, "col", -1)
-    p_top = shifted(bottom, "row", 1)
-    p_bottom = shifted(top, "row", -1)
-
-    base = (1 - parity) * lats
-    sources = jnp.stack([base + lats - steps, base, by_parity(lats - own, 0)]).astype(jnp.int32)
-    sources, top = lax.optimization_barrier((sources, top))
-    left_m, right_m = pack_mirror(covariance, sources, own, steps, nlon)
-    left_m, right_m, first_inner, wind_index, p_top, p_bottom = lax.optimization_barrier(
-        (left_m, right_m, first_inner, wind_index, p_top, p_bottom)
-    )
+    right = shifted(first, "col", -1)
     left_m = lax.ppermute(left_m, ("row", "col"), mirror_pairs(n_row, n_col, 1))
     right_m = lax.ppermute(right_m, ("row", "col"), mirror_pairs(n_row, n_col, -1))
-    right_inner = shifted(first_inner, "col", -1)
+    p_top = shifted(bottom, "row", 1)
+    p_top, top, wind_index = lax.optimization_barrier((p_top, top, wind_index))
+    p_bottom = shifted(top, "row", -1)
 
     weights = looked_up(wind_table, diffusivity, wind_index)
     padded_w = jnp.pad(weights, ((0, 0), (0, 0), (steps, steps)))
@@ -373,21 +339,26 @@
     col_w = lax.dynamic_slice_in_dim(padded_w, col_id * lats, lats + 2 * steps, 2).reshape(-1)
 
     operator_times_prior = rows_operator(covariance, p_top, p_bottom, row_w, steps, nlon, BF16)
-    operator_times_prior, right_outer = lax.optimization_barrier((operator_times_prior, right_outer))
+    operator_times_prior, left, right, first_inner, last_inner = lax.optimization_barrier(
+        (operator_times_prior, left, right, first_inner, last_inner)
+    )
+    left_inner = shifted(last_inner, "col", 1)
+    right_inner = shifted(first_inner, "col", -1)
     same = lambda i: i
     inner_at = lambda i, at: at[0] + i
     mirror, t_first, t_last = columns_operator(
-        covariance, left, right_outer, col_w, mirror_at, steps, nlon, 2 * near,
-        lambda i, at: edge_at(i, near, 2 * own), lambda i: edge_at(i, near, own), same,
+        covariance, left, right, col_w, mirror_at, steps, nlon, 2 * near,
+        lambda i, at: edge_at(i, near, 2 * own), same, same,
     )
     t_top = shifted(t_last, "row", 1)
+    t_first, left_m = lax.optimization_barrier((t_first, left_m))
     t_bottom = shifted(t_first, "row", -1)
     (mirror,) = columns_operator(
         covariance, left_m, right_m, col_w, mirror_at, steps, nlon, own, inner_at, same, same, mirror
     )
     (mirror,) = columns_operator(
-        covariance, left, right_inner, col_w, direct_at, steps, nlon, own, inner_at,
-        lambda i: i + near, same, mirror, 10 ** 13,
+        covariance, left_inner, right_inner, col_w, direct_at, steps, nlon, own, inner_at, same, same, mirror,
+        10 ** 13,
     )
     diagonal = (col_id * lats - row_id * lat_rows).astype(jnp.int32).reshape(1)
     predicted_spread_matrix = rows_operator(

time: 118 us -> 120 us (1.017)
  starting transfers between devices: 24.8 us -> 39.5 us
  waiting for transfers between devices: 19.7 us -> 12.8 us
  Pallas kernels: 69.4 us -> 62.7 us
    ppermute x7 -> x8, starting transfers between devices: 19.5 us -> 33.5 us  [shifted(): return lax.ppermute(block, axis, pairs)]
    ppermute x7 -> x8, waiting for transfers between devices: 19.6 us -> 12.7 us  [shifted(): return lax.ppermute(block, axis, pairs)]
    pallas_call x2 -> x1, Pallas kernels: 13.5 us -> 6.88 us  [pack(): pl.pallas_call(kernel, in_specs=[pl.BlockSpec(memory_space=pltpu.SMEM), p...]
  transfers between devices with their start and end apart: 9 -> 10, of which waited for: 2 -> 2; matrix products, arithmetic and copies ran while one was open for 2% -> 2% of each run, Pallas kernels for 38% -> 34%
where the time goes in v1:
time: 120 us; the launch traced here: 118 us
  Pallas kernels  62.7 us (52%)
  starting transfers between devices  39.5 us (33%)
  waiting for transfers between devices  12.8 us (11%)
  local copies, waits for them, and re-layouts  1.57 us (1%)
    ppermute x8, starting transfers between devices, shifted(): return lax.ppermute(block, axis, pairs)  33.5 us
    pallas_call x2, Pallas kernels, rows_operator(): pl.pallas_call(kernel, grid=(cols // nlon,), in_specs=in_specs, out_specs...  31.1 us
    pallas_call x3, Pallas kernels, columns_operator(): pl.pallas_call(kernel, grid_spec=pltpu.PrefetchScalarGridSpec(num_scalar_...  24.7 us
    ppermute x8, waiting for transfers between devices, shifted(): return lax.ppermute(block, axis, pairs)  12.7 us
    pallas_call x1, Pallas kernels, pack(): pl.pallas_call(kernel, in_specs=[pl.BlockSpec(memory_space=pltpu.SMEM), p...  6.88 us
    ppermute x1, starting transfers between devices, body(): lax.ppermute(right_m, ('row', 'col'), mirror_pairs(n_row, n_col, -1))  3.29 us
    ppermute x1, starting transfers between devices, body(): left_m = lax.ppermute(left_m, ('row', 'col'), mirror_pairs(n_row, n_col, 1))  2.71 us
  transfers between devices with their start and end apart: 10, of which 2 were waited for; matrix products, arithmetic and copies ran while one was open for 2% of the time, Pallas kernels for 34%

profile of v1, /device:TPU:5, one launch (start us, length us, event | category | flops | bytes accessed | tf_op | source)
XLA Modules:
  0.0 118.3 jit_solution(2647842896820538274)
XLA Ops:
  0.6 0.0 copy-start
  0.7 0.6 pad_add_fusion.where_ref
  1.3 0.0 copy-start.2
  1.3 0.0 copy-start.3
  1.3 6.9 %pack.1 = (bf16[1024,384]{1,0:T(8,128)(2,1)}, bf16[1024,384]{1,0:T(8,128)(2,1)}, bf16[512,384]{1,0:T(8,128)(2,1)}, bf16[512,384]{1,0:T(8,128)(2,1)}, bf16[512,38...) custom-call(s32[4]{0:T(128)} %pad_add_fusion.where_ref, ...), custom_call_target="tpu_custom_call" | custom-call | flops 1 | bytes 1 | tf_op jit(solution)/shard_map/pack/pallas_call | solution.py:139
  8.2 3.7 %collective-permute-start = (bf16[384,1024]{1,0:T(8,128)(2,1)}, bf16[384,1024]{1,0:T(8,128)(2,1)}, u32[]{:S(2)}, u32[]{:S(2)}) collective-permute-start(bf16[384,1024]{1,0:T(8,128)(2,1)} %get-tuple-element.23), channel_id=1, source_target_pairs={{0,8},{8,16},{16,24},{1,9},{9,17},{17,25},{2,10},{10,18},{18,26},{... | collective-permute-start | bytes 2359304 | tf_op jit(solution)/shard_map/ppermute | solution.py:278
  11.8 2.7 %collective-permute-start.6 = (bf16[512,384]{1,0:T(8,128)(2,1)}, bf16[512,384]{1,0:T(8,128)(2,1)}, u32[]{:S(2)}, u32[]{:S(2)}) collective-permute-start(bf16[512,384]{1,0:T(8,128)(2,1)} %get-tuple-element.37), channel_id=1, source_target_pairs={{0,2},{1,1},{2,10},{3,9},{4,18},{5,17},{6,26},{7,25},{8,4},{9,3},{... | collective-permute-start | bytes 1179656 | tf_op jit(solution)/shard_map/ppermute | solution.py:330
  14.6 3.3 %collective-permute-start.7 = (bf16[512,384]{1,0:T(8,128)(2,1)}, bf16[512,384]{1,0:T(8,128)(2,1)}, u32[]{:S(2)}, u32[]{:S(2)}) collective-permute-start(bf16[512,384]{1,0:T(8,128)(2,1)} %get-tuple-element.39), channel_id=1, source_target_pairs={{0,0},{2,8},{4,16},{6,24},{8,2},{9,1},{10,10},{11,9},{12,18},{13,1... | collective-permute-start | bytes 1179656 | tf_op jit(solution)/shard_map/ppermute | solution.py:331
  17.9 4.8 %collective-permute-start.2 = (bf16[1024,384]{1,0:T(8,128)(2,1)}, bf16[1024,384]{1,0:T(8,128)(2,1)S(1)}, u32[]{:S(2)}, u32[]{:S(2)}) collective-permute-start(bf16[1024,384]{1,0:T(8,128)(2,1)} %get-tuple-element.28), channel_id=1, source_target_pairs={{0,1},{1,2},{2,3},{3,4},{4,5},{5,6},{6,7},{8,9},{9,10},{10,11},{11... | collective-permute-start | bytes 2359304 | tf_op jit(solution)/shard_map/ppermute | solution.py:278
  22.7 1.9 %collective-permute-start.3 = (bf16[1024,384]{1,0:T(8,128)(2,1)}, bf16[1024,384]{1,0:T(8,128)(2,1)}, u32[]{:S(2)}, u32[]{:S(2)}) collective-permute-start(bf16[1024,384]{1,0:T(8,128)(2,1)} %get-tuple-element.29), channel_id=1, source_target_pairs={{1,0},{2,1},{3,2},{4,3},{5,4},{6,5},{7,6},{9,8},{10,9},{11,10},{12... | collective-permute-start | bytes 2359304 | tf_op jit(solution)/shard_map/ppermute | solution.py:278
  24.6 0.7 collective-permute-done.top_ref
  25.3 0.0 copy-done.2
  25.3 0.0 copy-done.3
  25.3 0.1 fusion
  25.5 0.0 copy-done
  25.5 0.1 fusion.1
  25.6 1.9 %collective-permute-start.1 = (bf16[384,1024]{1,0:T(8,128)(2,1)}, bf16[384,1024]{1,0:T(8,128)(2,1)}, u32[]{:S(2)}, u32[]{:S(2)}) collective-permute-start(bf16[384,1024]{1,0:T(8,128)(2,1)} %get-tuple-element.27), channel_id=1, source_target_pairs={{8,0},{16,8},{24,16},{9,1},{17,9},{25,17},{10,2},{18,10},{26,18},{... | collective-permute-start | bytes 2359304 | tf_op jit(solution)/shard_map/ppermute | solution.py:278
  27.6 0.1 pad_dynamic-slice_fusion.1
  27.7 0.7 reshape.18.weight_ref
  28.4 12.0 %collective-permute-done.1.bottom_ref = bf16[384,1024]{1,0:T(8,128)(2,1)} collective-permute-done((bf16[384,1024]{1,0:T(8,128)(2,1)}, bf16[384,1024]{1,0:T(8,128)(2,1)}, u32[]{:S(2)}, u32[]{:S(2)}) %collective-permute-start.1) | collective-permute-done | bytes 786464 | tf_op jit(solution)/shard_map/ppermute | solution.py:278
  40.4 15.7 %rows_operator.2 = bf16[2048,1024]{1,0:T(8,128)(2,1)} custom-call(f32[330]{0:T(512)} %reshape.18.weight_ref, f32[2048,1024]{1,0:T(8,128)} %p_ref.7, bf16[384,1024]{1,0:T(8,128)(2,1)} %collective-permute-done.top_ref, bf16[384,1024]{1,0:T(8,128)(2,1)} %collective-permute-done.1.bottom_ref), custom_call_target="tpu_custom_call" | custom-call | flops 1 | bytes 1 | tf_op jit(solution)/shard_map/rows_operator/pallas_call | solution.py:260
  56.1 0.0 collective-permute-done.2.left_ref
  56.1 0.0 copy-start.1
  56.1 0.0 collective-permute-done.3.right_ref
  56.1 13.7 %collective-permute-start.4 = (bf16[512,384]{1,0:T(8,128)(2,1)}, bf16[512,384]{1,0:T(8,128)(2,1)}, u32[]{:S(2)}, u32[]{:S(2)}) collective-permute-start(bf16[512,384]{1,0:T(8,128)(2,1)} %get-tuple-element.32), channel_id=1, source_target_pairs={{0,1},{1,2},{2,3},{3,4},{4,5},{5,6},{6,7},{8,9},{9,10},{10,11},{11... | collective-permute-start | bytes 1179656 | tf_op jit(solution)/shard_map/ppermute | solution.py:278
  69.8 1.9 %collective-permute-start.5 = (bf16[512,384]{1,0:T(8,128)(2,1)}, bf16[512,384]{1,0:T(8,128)(2,1)}, u32[]{:S(2)}, u32[]{:S(2)}) collective-permute-start(bf16[512,384]{1,0:T(8,128)(2,1)} %get-tuple-element.33), channel_id=1, source_target_pairs={{1,0},{2,1},{3,2},{4,3},{5,4},{6,5},{7,6},{9,8},{10,9},{11,10},{12... | collective-permute-start | bytes 1179656 | tf_op jit(solution)/shard_map/ppermute | solution.py:278
  71.8 0.1 pad_dynamic-slice_fusion
  71.9 0.7 reshape.20.weight_ref
  72.6 0.0 copy-done.1
  72.6 11.7 %columns_operator.3 = (bf16[2048,1024]{1,0:T(8,128)(2,1)}, bf16[384,1024]{1,0:T(8,128)(2,1)}, bf16[384,1024]{1,0:T(8,128)(2,1)}) custom-call(s32[1]{0:T(128)} %bitcast.where_ref, f32[210]{0:T(256)} %reshape.20.weight_ref, f32[2048,1024]{1,0:T(8,128)} %p_ref.7, bf16[1024,384]{1,0:T(8,128)(2,1)} %copy-done.1, bf16[1024,384]{1,0:T(8,128)(2,1)} %collective-permute-done.3.right_ref), custom_call_target="tpu_custom_call" | custom-call | flops 1 | bytes 1 | tf_op jit(solution)/shard_map/columns_operator/pallas_call | solution.py:203
  84.2 0.0 collective-permute-done.6.left_ref
  84.2 1.9 %collective-permute-start.9 = (bf16[384,1024]{1,0:T(8,128)(2,1)}, bf16[384,1024]{1,0:T(8,128)(2,1)}, u32[]{:S(2)}, u32[]{:S(2)}) collective-permute-start(bf16[384,1024]{1,0:T(8,128)(2,1)} %get-tuple-element.42), channel_id=1, source_target_pairs={{8,0},{16,8},{24,16},{9,1},{17,9},{25,17},{10,2},{18,10},{26,18},{... | collective-permute-start | bytes 2359304 | tf_op jit(solution)/shard_map/ppermute | solution.py:278
  86.2 3.6 %collective-permute-start.8 = (bf16[384,1024]{1,0:T(8,128)(2,1)}, bf16[384,1024]{1,0:T(8,128)(2,1)}, u32[]{:S(2)}, u32[]{:S(2)}) collective-permute-start(bf16[384,1024]{1,0:T(8,128)(2,1)} %get-tuple-element.41), channel_id=1, source_target_pairs={{0,8},{8,16},{16,24},{1,9},{9,17},{17,25},{2,10},{10,18},{18,26},{... | collective-permute-start | bytes 2359304 | tf_op jit(solution)/shard_map/ppermute | solution.py:278
  89.8 0.0 collective-permute-done.7.right_ref
  89.8 6.5 %columns_operator.4.rest_0_ = bf16[2048,1024]{1,0:T(8,128)(2,1)} custom-call(s32[1]{0:T(128)} %bitcast.where_ref, f32[210]{0:T(256)} %reshape.20.weight_ref, f32[2048,1024]{1,0:T(8,128)} %p_ref.7, bf16[512,384]{1,0:T(8,128)(2,1)} %collective-permute-done.6.left_ref, ...), custom_call_target="tpu_custom_call", output_to_operand_aliasing={{}: (5, {})} | custom-call | flops 1 | bytes 1 | tf_op jit(solution)/shard_map/columns_operator/pallas_call | solution.py:203
  96.3 0.0 collective-permute-done.4.left_ref
  96.3 0.0 collective-permute-done.5.right_ref
  96.3 6.5 %columns_operator.5.x_ref = bf16[2048,1024]{1,0:T(8,128)(2,1)} custom-call(s32[1]{0:T(128)} %bitcast.13.where_ref, f32[210]{0:T(256)} %reshape.20.weight_ref, f32[2048,1024]{1,0:T(8,128)} %p_ref.7, bf16[512,384]{1,0:T(8,128)(2,1)} %collective-permute-done.4.left_ref, ...), custom_call_target="tpu_custom_call", output_to_operand_aliasing={{}: (5, {})} | custom-call | flops 9999999827968 | bytes 9999999827968 | tf_op jit(solution)/shard_map/columns_operator/pallas_call | solution.py:203
  102.8 0.0 collective-permute-done.9.bottom_ref
  102.8 0.0 collective-permute-done.8.top_ref
  102.8 15.5 %rows_operator.3 = f32[2048,1024]{1,0:T(8,128)} custom-call(f32[330]{0:T(512)} %reshape.18.weight_ref, bf16[2048,1024]{1,0:T(8,128)(2,1)} %columns_operator.5.x_ref, bf16[384,1024]{1,0:T(8,128)(2,1)} %collective-permute-done.8.top_ref, bf16[384,1024]{1,0:T(8,128)(2,1)} %collective-permute-done.9.bottom_ref, s32[1]{0:T(128)} %bitcast.14.rest_0_, ...), custom_call_target="tpu_custom_call" | custom-call | flops 1 | bytes 1 | tf_op jit(solution)/shard_map/rows_operator/pallas_call | solution.py:260
  (6 shorter events, 0.1 us)
Async XLA Ops:
  0.6 24.8 %copy-start = (f32[16,2]{0,1:T(2,128)S(1)}, f32[16,2]{0,1:T(2,128)}, u32[]{:S(2)}) copy-start(f32[16,2]{0,1:T(2,128)} %param.7) | copy-start | bytes 388
  1.3 24.1 %copy-start.2 = (s32[3,64]{1,0:T(4,128)S(1)}, s32[3,64]{1,0:T(4,128)}, u32[]{:S(2)}) copy-start(s32[3,64]{1,0:T(4,128)} %param.9) | copy-start | bytes 2308
  1.3 24.1 %copy-start.3 = (f32[16]{0:T(128)S(1)}, f32[16]{0:T(128)}, u32[]{:S(2)}) copy-start(f32[16]{0:T(128)} %param.8) | copy-start | bytes 196
  8.2 17.2 %collective-permute-start = (bf16[384,1024]{1,0:T(8,128)(2,1)}, bf16[384,1024]{1,0:T(8,128)(2,1)}, u32[]{:S(2)}, u32[]{:S(2)}) collective-permute-start(bf16[384,1024]{1,0:T(8,128)(2,1)} %get-tuple-element.23), channel_id=1, source_target_pairs={{0,8},{8,16},{16,24},{1,9},{9,17},{17,25},{2,10},{10,18},{18,26},{... | collective-permute-start | bytes 2359304 | tf_op jit(solution)/shard_map/ppermute | solution.py:278
  11.8 72.4 %collective-permute-start.6 = (bf16[512,384]{1,0:T(8,128)(2,1)}, bf16[512,384]{1,0:T(8,128)(2,1)}, u32[]{:S(2)}, u32[]{:S(2)}) collective-permute-start(bf16[512,384]{1,0:T(8,128)(2,1)} %get-tuple-element.37), channel_id=1, source_target_pairs={{0,2},{1,1},{2,10},{3,9},{4,18},{5,17},{6,26},{7,25},{8,4},{9,3},{... | collective-permute-start | bytes 1179656 | tf_op jit(solution)/shard_map/ppermute | solution.py:330
  14.6 75.3 %collective-permute-start.7 = (bf16[512,384]{1,0:T(8,128)(2,1)}, bf16[512,384]{1,0:T(8,128)(2,1)}, u32[]{:S(2)}, u32[]{:S(2)}) collective-permute-start(bf16[512,384]{1,0:T(8,128)(2,1)} %get-tuple-element.39), channel_id=1, source_target_pairs={{0,0},{2,8},{4,16},{6,24},{8,2},{9,1},{10,10},{11,9},{12,18},{13,1... | collective-permute-start | bytes 1179656 | tf_op jit(solution)/shard_map/ppermute | solution.py:331
  17.9 38.2 %collective-permute-start.2 = (bf16[1024,384]{1,0:T(8,128)(2,1)}, bf16[1024,384]{1,0:T(8,128)(2,1)S(1)}, u32[]{:S(2)}, u32[]{:S(2)}) collective-permute-start(bf16[1024,384]{1,0:T(8,128)(2,1)} %get-tuple-element.28), channel_id=1, source_target_pairs={{0,1},{1,2},{2,3},{3,4},{4,5},{5,6},{6,7},{8,9},{9,10},{10,11},{11... | collective-permute-start | bytes 2359304 | tf_op jit(solution)/shard_map/ppermute | solution.py:278
  22.7 33.4 %collective-permute-start.3 = (bf16[1024,384]{1,0:T(8,128)(2,1)}, bf16[1024,384]{1,0:T(8,128)(2,1)}, u32[]{:S(2)}, u32[]{:S(2)}) collective-permute-start(bf16[1024,384]{1,0:T(8,128)(2,1)} %get-tuple-element.29), channel_id=1, source_target_pairs={{1,0},{2,1},{3,2},{4,3},{5,4},{6,5},{7,6},{9,8},{10,9},{11,10},{12... | collective-permute-start | bytes 2359304 | tf_op jit(solution)/shard_map/ppermute | solution.py:278
  25.6 14.8 %collective-permute-start.1 = (bf16[384,1024]{1,0:T(8,128)(2,1)}, bf16[384,1024]{1,0:T(8,128)(2,1)}, u32[]{:S(2)}, u32[]{:S(2)}) collective-permute-start(bf16[384,1024]{1,0:T(8,128)(2,1)} %get-tuple-element.27), channel_id=1, source_target_pairs={{8,0},{16,8},{24,16},{9,1},{17,9},{25,17},{10,2},{18,10},{26,18},{... | collective-permute-start | bytes 2359304 | tf_op jit(solution)/shard_map/ppermute | solution.py:278
  56.1 16.4 %copy-start.1 = (bf16[1024,384]{1,0:T(8,128)(2,1)}, bf16[1024,384]{1,0:T(8,128)(2,1)S(1)}, u32[]{:S(2)}) copy-start(bf16[1024,384]{1,0:T(8,128)(2,1)S(1)} %collective-permute-done.2.left_ref) | copy-start | bytes 2359300
  56.1 40.2 %collective-permute-start.4 = (bf16[512,384]{1,0:T(8,128)(2,1)}, bf16[512,384]{1,0:T(8,128)(2,1)}, u32[]{:S(2)}, u32[]{:S(2)}) collective-permute-start(bf16[512,384]{1,0:T(8,128)(2,1)} %get-tuple-element.32), channel_id=1, source_target_pairs={{0,1},{1,2},{2,3},{3,4},{4,5},{5,6},{6,7},{8,9},{9,10},{10,11},{11... | collective-permute-start | bytes 1179656 | tf_op jit(solution)/shard_map/ppermute | solution.py:278
  69.8 26.5 %collective-permute-start.5 = (bf16[512,384]{1,0:T(8,128)(2,1)}, bf16[512,384]{1,0:T(8,128)(2,1)}, u32[]{:S(2)}, u32[]{:S(2)}) collective-permute-start(bf16[512,384]{1,0:T(8,128)(2,1)} %get-tuple-element.33), channel_id=1, source_target_pairs={{1,0},{2,1},{3,2},{4,3},{5,4},{6,5},{7,6},{9,8},{10,9},{11,10},{12... | collective-permute-start | bytes 1179656 | tf_op jit(solution)/shard_map/ppermute | solution.py:278
  84.2 18.6 %collective-permute-start.9 = (bf16[384,1024]{1,0:T(8,128)(2,1)}, bf16[384,1024]{1,0:T(8,128)(2,1)}, u32[]{:S(2)}, u32[]{:S(2)}) collective-permute-start(bf16[384,1024]{1,0:T(8,128)(2,1)} %get-tuple-element.42), channel_id=1, source_target_pairs={{8,0},{16,8},{24,16},{9,1},{17,9},{25,17},{10,2},{18,10},{26,18},{... | collective-permute-start | bytes 2359304 | tf_op jit(solution)/shard_map/ppermute | solution.py:278
  86.2 16.6 %collective-permute-start.8 = (bf16[384,1024]{1,0:T(8,128)(2,1)}, bf16[384,1024]{1,0:T(8,128)(2,1)}, u32[]{:S(2)}, u32[]{:S(2)}) collective-permute-start(bf16[384,1024]{1,0:T(8,128)(2,1)} %get-tuple-element.41), channel_id=1, source_target_pairs={{0,8},{8,16},{16,24},{1,9},{9,17},{17,25},{2,10},{10,18},{18,26},{... | collective-permute-start | bytes 2359304 | tf_op jit(solution)/shard_map/ppermute | solution.py:278
